TPU v7x, 32 devices: a whole 2x2x4 slice. The times are simulated.
32 devices in a mesh: ctx: 8 (over z, x), kvh: 4 (over y, core).
Axes of the slice: x: 2, y: 2, z: 4, core: 2. Of those that a mesh axis runs over, the one named last changes fastest.
Arguments:
- queries: bfloat16 [3072, 4096], P('ctx', 'kvh'), may hold values from -110 to 110
- keys: bfloat16 [3072, 1024], P('ctx', 'kvh'), may hold values from -4.5 to 4.5
- values: bfloat16 [3072, 1024], P('ctx', 'kvh'), may hold values from -6 to 6
- vertical: int32 [8, 4], P('kvh'), may hold values from 0 to 47, as said below
- offsets: int32 [8, 3], P('kvh'), may hold values from 0 to 319, as said below
Outputs:
- attended: bfloat16 [3072, 4096], P(('ctx', 'kvh'))
Inputs may be any that keep to these rules, and one draw needn't show every extreme that they name: `vertical`: each entry names a block of 64 keys; the 4 blocks of one key-value head lie in distinct shards of 384 positions. `offsets`: entry 0 of every head is 0; the bands [o, o + 64) of one head are disjoint.
All inputs are finite; a program needn't handle non-finite values.
Results may differ from a plain program's by a relative error of at most 0.0044.
Values may be sent and summed in bfloat16 or wider, within the bound.
A program may use at most 128 MiB of HBM per device.

v0:
```python
import jax
import jax.numpy as jnp
from jax import lax
from jax.sharding import PartitionSpec as P

BLK = 64


NEG = -1e30


def shifted_2(shard, axis, by):
    devices = lax.axis_size(axis)
    pairs = [(i, i + by) for i in range(devices) if 0 <= i + by < devices]
    return lax.ppermute(shard, axis, pairs)


def band_tiles(window, begin, tok_rows, head_width):
    tile_count = tok_rows // BLK
    section = lax.dynamic_slice_in_dim(window, begin, tok_rows + BLK, 0)
    lower = section[:tok_rows].reshape(tile_count, BLK, head_width)
    upper = section[BLK:].reshape(tile_count, BLK, head_width)
    return jnp.concatenate([lower, upper], axis=1)


def attend(
    query_tile,
    first_pos,
    key_window,
    value_window,
    vert_keys,
    vert_values,
    vert_blocks,
    band_starts,
):
    tok_rows, group_size, head_width = query_tile.shape
    tile_count = tok_rows // BLK
    scaling = head_width ** (-0.5)
    query_pos = first_pos + jnp.arange(tok_rows, dtype=jnp.int32)
    vert_pos = (vert_blocks[:, None] * BLK + jnp.arange(BLK, dtype=jnp.int32)[None, :]).reshape(-1)
    distance = query_pos[:, None] - vert_pos[None, :]
    allowed = distance >= 0
    band_count = band_starts.shape[0]
    for band_num in range(band_count):
        shifted = distance - band_starts[band_num]
        allowed = allowed & ~((shifted >= 0) & (shifted < BLK))
    vert_scores = (
        jnp.einsum("qgd,kd->gqk", query_tile, vert_keys, preferred_element_type=jnp.float32)
        * scaling
    )
    vert_scores = jnp.where(allowed[None], vert_scores, NEG)
    begins = tok_rows - band_starts - BLK
    slash_keys = jnp.stack(
        [band_tiles(key_window, begins[b], tok_rows, head_width) for b in range(band_count)]
    )
    slash_values = jnp.stack(
        [band_tiles(value_window, begins[b], tok_rows, head_width) for b in range(band_count)]
    )
    query_blocks = query_tile.reshape(tile_count, BLK, group_size, head_width)
    slash_scores = (
        jnp.einsum("tagd,stcd->gstac", query_blocks, slash_keys, preferred_element_type=jnp.float32)
        * scaling
    )
    lag_rows = (
        jnp.arange(BLK, dtype=jnp.int32)[:, None]
        + BLK
        - jnp.arange(2 * BLK, dtype=jnp.int32)[None, :]
    )
    key_pos = (
        query_pos.reshape(tile_count, BLK)[None, :, :, None]
        - band_starts[:, None, None, None]
        - lag_rows[None, None]
    )
    band_mask = (lag_rows >= 0)[None, None] & (lag_rows < BLK)[None, None] & (key_pos >= 0)
    slash_scores = jnp.where(band_mask[None], slash_scores, NEG)
    row_top = jnp.maximum(
        vert_scores.max(axis=-1), slash_scores.max(axis=(1, 4)).reshape(group_size, tok_rows)
    )
    vert_exp = jnp.exp(vert_scores - row_top[:, :, None])
    slash_exp = jnp.exp(
        slash_scores - row_top.reshape(group_size, tile_count, BLK)[:, None, :, :, None]
    )
    totals = vert_exp.sum(axis=-1) + slash_exp.sum(axis=(1, 4)).reshape(group_size, tok_rows)
    vert_weights = vert_exp.astype(jnp.bfloat16)
    slash_weights = slash_exp.astype(jnp.bfloat16)
    blended = jnp.einsum(
        "gqk,kd->qgd", vert_weights, vert_values, preferred_element_type=jnp.float32
    )
    blended = blended + jnp.einsum(
        "gstac,stcd->tagd", slash_weights, slash_values, preferred_element_type=jnp.float32
    ).reshape(tok_rows, group_size, head_width)
    result = blended / totals.T[:, :, None]
    return result.astype(jnp.bfloat16).reshape(tok_rows, group_size * head_width)


def per_device(queries, keys, values, vertical, offsets):
    tok_rows = queries.shape[0]
    kv_heads = vertical.shape[0]
    head_width = keys.shape[1] // kv_heads
    group_size = queries.shape[1] // keys.shape[1]
    block_count = vertical.shape[1]
    per_shard = tok_rows // BLK
    shard_place = lax.axis_index("ctx")
    first_pos = shard_place * tok_rows
    earlier = shifted_2((keys, values), "ctx", 1)
    window_keys = jnp.concatenate([earlier[0], keys], axis=0)
    window_values = jnp.concatenate([earlier[1], values], axis=0)
    kv_local = jnp.stack(
        [
            keys.reshape(tok_rows, kv_heads, head_width),
            values.reshape(tok_rows, kv_heads, head_width),
        ],
        axis=0,
    )
    kv_local = kv_local.transpose(2, 0, 1, 3)
    owners = vertical // per_shard
    inside = vertical % per_shard
    mine = owners == shard_place
    offset_row = jnp.sum(jnp.where(mine, inside, 0), axis=1) * BLK
    present = jnp.any(mine, axis=1)
    slots = []
    for head_num in range(kv_heads):
        block_piece = lax.dynamic_slice_in_dim(kv_local[head_num], offset_row[head_num], BLK, 1)
        slots.append(jnp.where(present[head_num], block_piece, jnp.zeros_like(block_piece)))
    buffer = jnp.stack(slots)[None]
    gathered = lax.all_gather(buffer, "ctx", axis=0, tiled=True)
    fetched = []
    for head_num in range(kv_heads):
        picked = jnp.take(gathered[:, head_num], owners[head_num], axis=0)
        fetched.append(picked.transpose(1, 0, 2, 3).reshape(2, block_count * BLK, head_width))
    stored = jnp.stack(fetched)
    outputs = []
    query_heads = queries.reshape(tok_rows, kv_heads, group_size, head_width)
    for head_num in range(kv_heads):
        low = head_num * head_width
        outputs.append(
            attend(
                query_heads[:, head_num],
                first_pos,
                window_keys[:, low : low + head_width],
                window_values[:, low : low + head_width],
                stored[head_num, 0],
                stored[head_num, 1],
                vertical[head_num],
                offsets[head_num],
            )
        )
    joined = jnp.concatenate(outputs, axis=1)
    return lax.all_to_all(joined, "kvh", split_axis=0, concat_axis=1, tiled=True)


def solution(mesh):
    placed = (P("ctx", "kvh"), P("ctx", "kvh"), P("ctx", "kvh"), P("kvh", None), P("kvh", None))
    return jax.shard_map(
        per_device, mesh=mesh, in_specs=placed, out_specs=P(("ctx", "kvh"), None), check_vma=False
    )
```

profile of v0, /device:TPU:0, one launch (start us, length us, event | category | flops | bytes accessed | tf_op | source)
XLA Modules:
  0.0 119.6 jit_solution(2711621478897860869)
XLA Ops:
  0.0 4.8 %collective-permute-start = (bf16[384,256]{1,0:T(8,128)(2,1)}, bf16[384,256]{1,0:T(8,128)(2,1)S(1)}, u32[]{:S(2)}, u32[]{:S(2)}) collective-permute-start(bf16[384,256]{1,0:T(8,128)(2,1)} %param.8), channel_id=1, source_target_pairs={{0,4},{4,8},{8,12},{12,16},{16,20},{20,24},{24,28},{1,5},{5,9},{9,... | collective-permute-start | bytes 589832 | tf_op jit(solution)/shard_map/ppermute | solution.py:15
  4.9 3.5 %collective-permute-start.1 = (bf16[384,256]{1,0:T(8,128)(2,1)}, bf16[384,256]{1,0:T(8,128)(2,1)S(1)}, u32[]{:S(2)}, u32[]{:S(2)}) collective-permute-start(bf16[384,256]{1,0:T(8,128)(2,1)} %param.9), channel_id=1, source_target_pairs={{0,4},{4,8},{8,12},{12,16},{16,20},{20,24},{24,28},{1,5},{5,9},{9,... | collective-permute-start | bytes 589832 | tf_op jit(solution)/shard_map/ppermute | solution.py:15
  8.3 0.8 broadcast_subtract_fusion.3
  9.1 0.7 fusion.106
  13.5 0.8 slice_bitcast_fusion.11
  14.5 0.8 fusion.98
  15.3 0.8 fusion.89
  16.1 0.6 fusion.108
  19.2 1.1 copy.89
  20.3 1.1 copy.90
  21.4 1.6 %fusion.105 = (s32[1,1]{1,0:T(1,128)}, s32[1,1]{1,0:T(1,128)}, s32[1,1]{1,0:T(1,128)}, s32[1,1]{1,0:T(1,128)}, s32[1,1]{1,0:T(1,128)}, /*index=5*/s32[1,1]{1,0:T(1,128)}) fusion(s32[2,3]{1,0:T(2,128)} %param.11), kind=kLoop, calls=%fused_computation.210 | loop fusion | bytes 48 | tf_op jit(solution)/shard_map/slice | solution.py:45
  23.0 0.8 multiply_bitcast_fusion.1
  29.4 1.5 %copy.93 = bf16[384,1024]{0,1:T(8,128)(2,1)S(1)} copy(bf16[384,1024]{1,0:T(8,128)(2,1)} %param.7) | data formatting | bytes 1572864 | tf_op args[0]
  30.9 0.1 fusion.101
  30.9 0.9 copy.136
  31.9 0.6 fusion.107
  33.8 1.4 %dynamic-slice_select_fusion = (bf16[1,2,64,128]{2,3,0,1:T(8,128)(2,1)S(1)}, bf16[1,2,64,128]{2,3,0,1:T(8,128)(2,1)S(1)}) fusion(bf16[1,2,384,128]{2,3,0,1:T(8,128)(2,1)S(1)} %get-tuple-element.21, s32[]{:T(128)S(6)} %select_n.90, pred[]{:T(512)} %bitcast.6, bf16[1,2,384,128]{2,3,0,1:T(8,128)(2,1)S(1)} %get-tuple-element.20, s32[]{:T(128)S(6)} %select_n.87, ...), kind=kLoop, calls=%fused_computation.133 | loop fusion | flops 32768 | bytes 131082 | tf_op jit(solution)/shard_map/jit(_where)/select_n | solution.py:124
  35.2 32.9 %all-gather = bf16[16,2,64,128]{2,3,0,1:T(8,128)(2,1)S(1)} all-gather(bf16[2,2,64,128]{2,3,0,1:T(8,128)(2,1)S(1)} %pad_maximum_fusion.1), channel_id=2, replica_groups=mesh['ctx'=8,'kvh'=4] {'ctx'}, dimensions={0}, use_global_device_ids=true | all-gather | bytes 589824 | tf_op jit(solution)/shard_map/all_gather | solution.py:126
  68.2 0.4 copy.91
  68.6 0.6 gather_fusion
  69.2 0.1 select_bitcast_fusion.1
  69.4 0.1 add.143
  69.5 4.4 %fusion.81 = (pred[384,256]{0,1:T(8,128)(4,1)S(1)}, pred[384,256]{0,1:T(8,128)(4,1)S(1)}) fusion(s32[]{:T(128)} %bitcast.17, s32[]{:T(128)} %bitcast.16, s32[]{:T(128)} %bitcast.15, s32[256]{0:T(256)S(1)} %add.143, s32[384]{0:T(512)S(1)} %iota_add_fusion.2, s32[]{:T(128)} %bitcast.67, s32[]{:T(128)} %bitcast.66, s32[]{:T(128)} %bitcast.65, s32[256]{0:T(256)S(1)} %add.155), kind=kLoop, calls=%fused_computation.105 | loop fusion | flops 3932160 | bytes 200216 | tf_op jit(solution)/shard_map/and | solution.py:46
  73.9 1.5 %fusion.111 = (f32[4,384]{1,0:T(4,128)S(1)}, f32[4,384,256]{1,2,0:T(8,128)}) fusion(bf16[384,2,4,128]{0,3,2,1:T(8,128)(2,1)S(1)} %bitcast.230, bf16[1,2,256,128]{3,2,1,0:T(8,128)(2,1)S(1)} %bitcast.266, pred[384,256]{0,1:T(8,128)(4,1)S(1)} %get-tuple-element.50), kind=kOutput, calls=%fused_computation.216 | convolution fusion | flops 101841408 | bytes 2136064 | tf_op jit(solution)/shard_map/qgd,kd->gqk/dot_general | solution.py:48
  77.4 0.9 copy.137
  78.3 0.6 gather_fusion.1
  78.9 0.1 select_bitcast_fusion
  79.0 0.4 fusion.110
  79.6 1.1 fusion.52
  80.8 0.2 constant_dynamic-slice_fusion.11
  81.1 0.7 copy-done.9
  81.8 0.6 fusion.4
  82.4 1.4 %copy-done.1 = f32[6,3,128,64,4]{2,3,4,1,0:T(8,128)} copy-done((f32[6,3,128,64,4]{2,3,4,1,0:T(8,128)}, f32[6,3,128,64,4]{2,3,4,1,0:T(8,128)S(1)}, u32[]{:S(2)}) %copy-start.1) | copy-done | bytes 2359320
  83.8 0.9 fusion
  84.7 0.7 reshape.379
  85.5 0.6 max.26
  86.2 0.2 constant_dynamic-slice_fusion.8
  86.4 1.4 %copy-done.2 = f32[6,3,128,64,4]{2,3,4,1,0:T(8,128)S(1)} copy-done((f32[6,3,128,64,4]{2,3,4,1,0:T(8,128)S(1)}, f32[6,3,128,64,4]{2,3,4,1,0:T(8,128)}, u32[]{:S(2)}) %copy-start.2) | copy-done | bytes 2359320
  87.8 0.8 convolution_bitcast_fusion.1
  88.7 0.9 copy.101
  89.6 2.3 %copy.102 = f32[384,4,128]{0,2,1:T(8,128)} copy(f32[384,4,128]{2,0,1:T(8,128)} %bitcast.232) | data formatting | bytes 1572864 | tf_op jit(solution)/shard_map/reshape | solution.py:91
  91.9 1.0 fusion.6
  92.9 0.1 copy-done.5
  93.1 1.2 fusion.15
  94.2 1.2 %copy.104 = bf16[384,4,128]{2,1,0:T(4,128)(2,1)S(1)} copy(bf16[384,4,128]{0,2,1:T(8,128)(2,1)} %fusion.15) | data formatting | bytes 786432 | tf_op jit(solution)/shard_map/convert_element_type | solution.py:93
  95.5 0.2 concatenate.58
  95.6 0.2 constant_dynamic-slice_fusion.5
  95.9 0.5 copy-done.8
  96.4 0.2 copy-done.10
  96.5 0.6 fusion.5
  97.2 1.4 %copy-done.3 = f32[6,3,128,64,4]{2,3,4,1,0:T(8,128)} copy-done((f32[6,3,128,64,4]{2,3,4,1,0:T(8,128)}, f32[6,3,128,64,4]{2,3,4,1,0:T(8,128)S(1)}, u32[]{:S(2)}) %copy-start.3) | copy-done | bytes 2359320
  98.6 0.9 fusion.2
  99.7 0.2 constant_dynamic-slice_fusion.2
  99.9 1.4 %copy-done.4 = f32[6,3,128,64,4]{2,3,4,1,0:T(8,128)S(1)} copy-done((f32[6,3,128,64,4]{2,3,4,1,0:T(8,128)S(1)}, f32[6,3,128,64,4]{2,3,4,1,0:T(8,128)}, u32[]{:S(2)}) %copy-start.4) | copy-done | bytes 2359320
  101.3 0.8 convolution_bitcast_fusion
  102.3 0.3 copy.114
  102.6 0.2 fusion.8
  102.8 0.7 copy-done.12
  103.4 0.4 fusion.14
  103.9 0.2 copy.116
  104.1 0.2 concatenate.65
  104.3 0.1 pad_maximum_fusion
  104.4 14.2 %all_to_all.16 = bf16[4,96,1024]{2,1,0:T(8,128)(2,1)S(1)} all-to-all(bf16[4,96,1024]{2,1,0:T(8,128)(2,1)S(1)} %pad_maximum_fusion), channel_id=1, replica_groups=mesh['ctx'=8,'kvh'=4] {'kvh'}, dimensions={0} | all-to-all | bytes 1572864 | tf_op jit(solution)/shard_map/all_to_all | solution.py:149
  118.6 0.9 copy.138
  (81 shorter events, 1.5 us)
Async XLA Ops:
  0.0 80.7 %collective-permute-start = (bf16[384,256]{1,0:T(8,128)(2,1)}, bf16[384,256]{1,0:T(8,128)(2,1)S(1)}, u32[]{:S(2)}, u32[]{:S(2)}) collective-permute-start(bf16[384,256]{1,0:T(8,128)(2,1)} %param.8), channel_id=1, source_target_pairs={{0,4},{4,8},{8,12},{12,16},{16,20},{20,24},{24,28},{1,5},{5,9},{9,... | collective-permute-start | bytes 589832 | tf_op jit(solution)/shard_map/ppermute | solution.py:15
  4.9 81.2 %collective-permute-start.1 = (bf16[384,256]{1,0:T(8,128)(2,1)}, bf16[384,256]{1,0:T(8,128)(2,1)S(1)}, u32[]{:S(2)}, u32[]{:S(2)}) collective-permute-start(bf16[384,256]{1,0:T(8,128)(2,1)} %param.9), channel_id=1, source_target_pairs={{0,4},{4,8},{8,12},{12,16},{16,20},{20,24},{24,28},{1,5},{5,9},{9,... | collective-permute-start | bytes 589832 | tf_op jit(solution)/shard_map/ppermute | solution.py:15
  69.3 9.0 %copy-start.13 = (bf16[2,4,64,128]{3,2,1,0:T(8,128)(2,1)}, bf16[2,4,64,128]{3,2,1,0:T(8,128)(2,1)S(1)}, u32[]{:S(2)}) copy-start(bf16[2,4,64,128]{3,2,1,0:T(8,128)(2,1)S(1)} %copy.92) | copy-start | bytes 393220
  79.0 1.8 %copy-start.6 = (bf16[384,256]{1,0:T(8,128)(2,1)S(1)}, bf16[384,256]{1,0:T(8,128)(2,1)}, u32[]{:S(2)}) copy-start(bf16[384,256]{1,0:T(8,128)(2,1)} %param.8) | copy-start | bytes 589828
  79.0 1.7 %copy-start.11 = (bf16[2,4,64,128]{3,2,1,0:T(8,128)(2,1)}, bf16[2,4,64,128]{3,2,1,0:T(8,128)(2,1)S(1)}, u32[]{:S(2)}) copy-start(bf16[2,4,64,128]{3,2,1,0:T(8,128)(2,1)S(1)} %copy.105) | copy-start | bytes 393220
  79.4 1.4 %copy-start.15 = (f32[4,384]{1,0:T(4,128)}, f32[4,384]{1,0:T(4,128)S(1)}, u32[]{:S(2)}) copy-start(f32[4,384]{1,0:T(4,128)S(1)} %get-tuple-element.78) | copy-start | bytes 18436
  80.8 1.0 copy-start.9
  82.4 1.4 %copy-start.1 = (f32[6,3,128,64,4]{2,3,4,1,0:T(8,128)}, f32[6,3,128,64,4]{2,3,4,1,0:T(8,128)S(1)}, u32[]{:S(2)}) copy-start(f32[6,3,128,64,4]{2,3,4,1,0:T(8,128)S(1)} %get-tuple-element.81) | copy-start | bytes 7077892
  82.4 3.7 %copy-start.7 = (bf16[384,256]{1,0:T(8,128)(2,1)S(1)}, bf16[384,256]{1,0:T(8,128)(2,1)}, u32[]{:S(2)}) copy-start(bf16[384,256]{1,0:T(8,128)(2,1)} %param.9) | copy-start | bytes 589828
  86.1 1.7 %copy-start.2 = (f32[6,3,128,64,4]{2,3,4,1,0:T(8,128)S(1)}, f32[6,3,128,64,4]{2,3,4,1,0:T(8,128)}, u32[]{:S(2)}) copy-start(f32[6,3,128,64,4]{2,3,4,1,0:T(8,128)} %copy-done.1) | copy-start | bytes 7077892
  88.7 3.2 %copy-start = (f32[4,384,256]{1,2,0:T(8,128)S(1)}, f32[4,384,256]{1,2,0:T(8,128)}, u32[]{:S(2)}) copy-start(f32[4,384,256]{1,2,0:T(8,128)} %get-tuple-element.83) | copy-start | bytes 4718596
  91.9 1.0 copy-start.18
  91.9 1.2 copy-start.5
  91.9 1.2 copy-start.14
  91.9 1.2 copy-start.17
  95.5 0.9 copy-start.8
  95.5 1.1 copy-start.10
  97.2 1.4 %copy-start.3 = (f32[6,3,128,64,4]{2,3,4,1,0:T(8,128)}, f32[6,3,128,64,4]{2,3,4,1,0:T(8,128)S(1)}, u32[]{:S(2)}) copy-start(f32[6,3,128,64,4]{2,3,4,1,0:T(8,128)S(1)} %get-tuple-element.77) | copy-start | bytes 7077892
  97.2 2.5 %copy-start.16 = (f32[4,384]{1,0:T(4,128)S(1)}, f32[4,384]{1,0:T(4,128)}, u32[]{:S(2)}) copy-start(f32[4,384]{1,0:T(4,128)} %copy-done.15) | copy-start | bytes 18436
  99.7 1.7 %copy-start.4 = (f32[6,3,128,64,4]{2,3,4,1,0:T(8,128)S(1)}, f32[6,3,128,64,4]{2,3,4,1,0:T(8,128)}, u32[]{:S(2)}) copy-start(f32[6,3,128,64,4]{2,3,4,1,0:T(8,128)} %copy-done.3) | copy-start | bytes 7077892
  102.5 0.9 copy-start.12
where the time goes:
time: 120 us
  blocking collectives  47.2 us (39%)
  local copies, waits for them, and re-layouts  27.5 us (23%)
  between operations  15.6 us (13%)
  other arithmetic  14.5 us (12%)
  starting transfers between devices  8.3 us (7%)
  matrix products  6.45 us (5%)
    all_gather x1, blocking collectives, per_device(): gathered = lax.all_gather(buffer, 'ctx', axis=0, tiled=True)  32.9 us
    all_to_all x1, blocking collectives, per_device(): lax.all_to_all(joined, 'kvh', split_axis=0, concat_axis=1, tiled=True)  14.2 us
    unnamed x45, local copies, waits for them, and re-layouts  13.3 us
    ppermute x2, starting transfers between devices, shifted_2(): return lax.ppermute(shard, axis, pairs)  8.3 us
    and x1, other arithmetic, attend(): allowed = allowed & ~((shifted >= 0) & (shifted < BLK))  4.37 us
    reshape x2, local copies, waits for them, and re-layouts, attend(): blended = blended + jnp.einsum('gstac,stcd->tagd', slash_weights, slash_v...  2.55 us
  transfers between devices with their start and end apart: 2, of which 0 were waited for; matrix products, arithmetic and copies ran while one was open for 23% of the time, Pallas kernels for 0%

commit v1 on v0

v1 whole, which is shorter than its diff:
```python
import functools
import math

import jax
import jax.numpy as jnp
from jax import lax
from jax.experimental import pallas as pl
from jax.experimental.pallas import tpu as pltpu
from jax.sharding import PartitionSpec as P

BLK = 64
NEG = -1e30
MESH = pl.DeviceIdType.MESH


def each(count, body):
    if count <= 16:
        for i in range(count):
            body(i)
    else:
        lax.fori_loop(0, count, lambda i, carry: (body(i), carry)[1], 0)


def kernel(
    n_ctx,
    n_kvh,
    vert_ref,
    offs_ref,
    q_ref,
    k_ref,
    v_ref,
    out_ref,
    k_prev,
    v_prev,
    gath,
    obuf,
    kv_send,
    kv_recv,
    vert_send,
    vert_recv,
    out_send,
    out_recv,
    out_local,
):
    c = lax.axis_index("ctx")
    me = lax.axis_index("kvh")
    tok = q_ref.shape[0]
    heads = vert_ref.shape[0]
    slots = vert_ref.shape[1]
    bands = offs_ref.shape[1]
    hd = k_ref.shape[1] // heads
    group = q_ref.shape[1] // k_ref.shape[1]
    gcols = group * hd
    rows = tok // n_kvh
    span = rows + tok
    per_shard = tok // BLK

    def ctx_peer(i):
        return lax.rem(c + 1 + i, n_ctx)

    barrier = pltpu.get_barrier_semaphore()
    each(
        n_ctx - 1,
        lambda i: pl.semaphore_signal(
            barrier, inc=1, device_id={"ctx": ctx_peer(i)}, device_id_type=MESH
        ),
    )
    for i in range(n_kvh - 1):
        pl.semaphore_signal(
            barrier,
            inc=1,
            device_id={"kvh": lax.rem(me + 1 + i, n_kvh)},
            device_id_type=MESH,
        )

    for g in range(heads):
        row = jnp.int32(0)
        for j in range(slots):
            block = vert_ref[g, j]
            away = lax.div(block, per_shard) - c
            row = row + lax.rem(block, per_shard) * (1 - jnp.minimum(away * away, 1))
        row = row * BLK
        cols = slice(g * hd, (g + 1) * hd)
        gath[c, g, 0] = k_ref[pl.ds(row, BLK), cols]
        gath[c, g, 1] = v_ref[pl.ds(row, BLK), cols]

    pl.semaphore_wait(barrier, n_ctx - 1 + n_kvh - 1)

    def vert_copy(i):
        peer = ctx_peer(i)
        return pltpu.make_async_remote_copy(
            src_ref=gath.at[c],
            dst_ref=gath.at[c],
            send_sem=vert_send.at[peer],
            recv_sem=vert_recv.at[c],
            device_id={"ctx": peer},
            device_id_type=MESH,
        )

    def vert_arrival(i):
        peer = ctx_peer(i)
        return pltpu.make_async_remote_copy(
            src_ref=gath.at[peer],
            dst_ref=gath.at[peer],
            send_sem=vert_send.at[peer],
            recv_sem=vert_recv.at[peer],
            device_id={"ctx": peer},
            device_id_type=MESH,
        )

    def kv_copy(which, chunk):
        src, dst = ((k_ref, k_prev), (v_ref, v_prev))[which]
        part = pl.ds(chunk * rows, rows)
        return pltpu.make_async_remote_copy(
            src_ref=src.at[part],
            dst_ref=dst.at[part],
            send_sem=kv_send.at[which, chunk],
            recv_sem=kv_recv.at[which, chunk],
            device_id={"ctx": lax.rem(c + 1, n_ctx)},
            device_id_type=MESH,
        )

    each(n_ctx - 1, lambda i: vert_copy(i).start())

    @pl.when(c < n_ctx - 1)
    def _():
        for chunk in reversed(range(n_kvh)):
            for which in range(2):
                kv_copy(which, chunk).start()

    @pl.when(c == 0)
    def _():
        k_prev[...] = jnp.zeros_like(k_prev)
        v_prev[...] = jnp.zeros_like(v_prev)

    lag = (
        lax.broadcasted_iota(jnp.int32, (rows, span), 0)
        + tok
        - lax.broadcasted_iota(jnp.int32, (rows, span), 1)
    )
    window_col = lax.broadcasted_iota(jnp.int32, (rows, span), 1)
    vert_lane = lax.broadcasted_iota(jnp.int32, (1, slots * BLK), 1)
    vert_row = lax.broadcasted_iota(jnp.int32, (rows, slots * BLK), 0)

    def in_bands(distance, g):
        found = None
        for s in range(bands):
            gap = distance - offs_ref[g, s]
            hit = (gap >= 0) & (gap < BLK)
            found = hit if found is None else found | hit
        return found

    each(n_ctx - 1, lambda i: vert_arrival(i).wait_recv())

    vert_k, vert_v, vert_pos = [], [], []
    for g in range(heads):
        owners = [lax.div(vert_ref[g, j], per_shard) for j in range(slots)]
        vert_k.append(jnp.concatenate([gath[o, g, 0] for o in owners], axis=0))
        vert_v.append(jnp.concatenate([gath[o, g, 1] for o in owners], axis=0))
        first = jnp.zeros_like(vert_lane)
        for j in range(slots):
            first = jnp.where(vert_lane // BLK == j, vert_ref[g, j], first)
        vert_pos.append(first * BLK + vert_lane % BLK)

    factor = math.log2(math.e) * hd**-0.5

    def out_copy(tile, g):
        return pltpu.make_async_remote_copy(
            src_ref=obuf.at[pl.ds(tile * rows, rows), pl.ds(g * gcols, gcols)],
            dst_ref=out_ref.at[
                :, pl.ds(pl.multiple_of(me * heads * gcols + g * gcols, gcols), gcols)
            ],
            send_sem=out_send.at[tile, g],
            recv_sem=out_recv.at[me, g],
            device_id={"kvh": tile},
            device_id_type=MESH,
        )

    def out_own(tile, g):
        return pltpu.make_async_copy(
            obuf.at[pl.ds(tile * rows, rows), pl.ds(g * gcols, gcols)],
            out_ref.at[
                :, pl.ds(pl.multiple_of(me * heads * gcols + g * gcols, gcols), gcols)
            ],
            out_local.at[g],
        )

    def out_arrival(peer, g):
        return pltpu.make_async_remote_copy(
            src_ref=obuf.at[pl.ds(0, rows), pl.ds(g * gcols, gcols)],
            dst_ref=out_ref.at[:, pl.ds(peer * heads * gcols + g * gcols, gcols)],
            send_sem=out_send.at[peer, g],
            recv_sem=out_recv.at[peer, g],
            device_id={"kvh": peer},
            device_id_type=MESH,
        )

    for tile in reversed(range(n_kvh)):
        base = tile * rows

        @pl.when(c > 0)
        def _():
            for which in range(2):
                kv_copy(which, tile).wait_recv()

        before = jnp.where(c == 0, tok - base, 0)
        for g in range(heads):
            cols = slice(g * hd, (g + 1) * hd)
            q = jnp.concatenate(
                [
                    q_ref[base : base + rows, (g * group + h) * hd : (g * group + h + 1) * hd]
                    for h in range(group)
                ],
                axis=0,
            )
            keys = jnp.concatenate([k_prev[base:, cols], k_ref[: base + rows, cols]], axis=0)
            vals = jnp.concatenate([v_prev[base:, cols], v_ref[: base + rows, cols]], axis=0)
            dims = (((1,), (1,)), ((), ()))
            score_w = lax.dot_general(q, keys, dims, preferred_element_type=jnp.float32)
            score_v = lax.dot_general(q, vert_k[g], dims, preferred_element_type=jnp.float32)
            mask_w = in_bands(lag, g) & (window_col >= before)
            vert_lag = vert_row + (c * tok + base) - vert_pos[g]
            mask_v = (vert_lag >= 0) & ~in_bands(vert_lag, g)
            score_w = jnp.where(mask_w[None], score_w.reshape(group, rows, span), NEG)
            score_v = jnp.where(mask_v[None], score_v.reshape(group, rows, slots * BLK), NEG)
            top = jnp.maximum(
                jnp.max(score_w, axis=-1, keepdims=True), jnp.max(score_v, axis=-1, keepdims=True)
            )
            exp_w = jnp.exp2((score_w - top) * factor)
            exp_v = jnp.exp2((score_v - top) * factor)
            total = jnp.sum(exp_w, axis=-1, keepdims=True) + jnp.sum(exp_v, axis=-1, keepdims=True)
            blended = jnp.dot(
                exp_w.astype(jnp.bfloat16).reshape(group * rows, span),
                vals,
                preferred_element_type=jnp.float32,
            ) + jnp.dot(
                exp_v.astype(jnp.bfloat16).reshape(group * rows, slots * BLK),
                vert_v[g],
                preferred_element_type=jnp.float32,
            )
            result = (blended.reshape(group, rows, hd) / total).astype(jnp.bfloat16)
            for h in range(group):
                obuf[base : base + rows, (g * group + h) * hd : (g * group + h + 1) * hd] = result[h]

            @pl.when(tile != me)
            def _():
                out_copy(tile, g).start()

            @pl.when(tile == me)
            def _():
                out_own(tile, g).start()

    each(n_ctx - 1, lambda i: vert_copy(i).wait_send())

    @pl.when(c < n_ctx - 1)
    def _():
        for chunk in range(n_kvh):
            for which in range(2):
                kv_copy(which, chunk).wait_send()

    for peer in range(n_kvh):
        for g in range(heads):

            @pl.when(peer != me)
            def _():
                out_copy(peer, g).wait_send()
                out_arrival(peer, g).wait_recv()

            @pl.when(peer == me)
            def _():
                out_own(peer, g).wait()


def per_device(n_ctx, n_kvh, queries, keys, values, vertical, offsets):
    tok = queries.shape[0]
    heads = vertical.shape[0]
    hd = keys.shape[1] // heads
    rows = tok // n_kvh
    vmem = pl.BlockSpec(memory_space=pltpu.VMEM)
    smem = pl.BlockSpec(memory_space=pltpu.SMEM)
    dma = pltpu.SemaphoreType.DMA
    return pl.pallas_call(
        functools.partial(kernel, n_ctx, n_kvh),
        out_shape=jax.ShapeDtypeStruct((rows, queries.shape[1] * n_kvh), jnp.bfloat16),
        in_specs=[smem, smem, vmem, vmem, vmem],
        out_specs=pl.BlockSpec(memory_space=pl.ANY),
        scratch_shapes=[
            pltpu.VMEM(keys.shape, jnp.bfloat16),
            pltpu.VMEM(values.shape, jnp.bfloat16),
            pltpu.VMEM((n_ctx, heads, 2, BLK, hd), jnp.bfloat16),
            pltpu.VMEM(queries.shape, jnp.bfloat16),
            dma((2, n_kvh)),
            dma((2, n_kvh)),
            dma((n_ctx,)),
            dma((n_ctx,)),
            dma((n_kvh, heads)),
            dma((n_kvh, heads)),
            dma((heads,)),
        ],
        compiler_params=pltpu.CompilerParams(
            collective_id=0, has_side_effects=True, vmem_limit_bytes=48 * 1024 * 1024
        ),
    )(vertical, offsets, queries, keys, values)


def solution(mesh):
    placed = (P("ctx", "kvh"), P("ctx", "kvh"), P("ctx", "kvh"), P("kvh", None), P("kvh", None))
    return jax.shard_map(
        functools.partial(per_device, mesh.shape["ctx"], mesh.shape["kvh"]),
        mesh=mesh,
        in_specs=placed,
        out_specs=P(("ctx", "kvh"), None),
        check_vma=False,
    )
```

time: 120 us -> 39.3 us (0.33)
  the two profiles are of different devices: /device:TPU:0 before, /device:TPU:16 now
where the time goes in v1:
time: 39.3 us; the launch traced here: 39 us
  Pallas kernels  33.8 us (86%)
  local copies, waits for them, and re-layouts  5.22 us (13%)
    pallas_call x1, Pallas kernels, per_device(): pl.pallas_call(functools.partial(kernel, n_ctx, n_kvh), out_shape=jax.Sha...  33.8 us
    unnamed x11, local copies, waits for them, and re-layouts  5.22 us

profile of v1, /device:TPU:16, one launch (start us, length us, event | category | flops | bytes accessed | tf_op | source)
XLA Modules:
  0.0 39.0 jit_solution(6383647221071363853)
XLA Ops:
  0.0 0.0 copy-start
  0.0 1.1 %copy-done = bf16[384,1024]{1,0:T(8,128)(2,1)S(1)} copy-done((bf16[384,1024]{1,0:T(8,128)(2,1)S(1)}, bf16[384,1024]{1,0:T(8,128)(2,1)}, u32[]{:S(2)}) %copy-start) | copy-done | bytes 786456
  1.1 0.0 copy-start.1
  1.1 0.9 %copy-done.1 = bf16[384,256]{1,0:T(8,128)(2,1)S(1)} copy-done((bf16[384,256]{1,0:T(8,128)(2,1)S(1)}, bf16[384,256]{1,0:T(8,128)(2,1)}, u32[]{:S(2)}) %copy-start.1) | copy-done | bytes 196632
  2.1 0.0 copy-start.2
  2.1 0.9 %copy-done.2 = bf16[384,256]{1,0:T(8,128)(2,1)S(1)} copy-done((bf16[384,256]{1,0:T(8,128)(2,1)S(1)}, bf16[384,256]{1,0:T(8,128)(2,1)}, u32[]{:S(2)}) %copy-start.2) | copy-done | bytes 196632
  3.0 0.0 copy-start.3
  3.0 0.7 %copy-done.3 = s32[2,4]{1,0:T(2,128)S(1)} copy-done((s32[2,4]{1,0:T(2,128)S(1)}, s32[2,4]{1,0:T(2,128)}, u32[]{:S(2)}) %copy-start.3) | copy-done | bytes 56
  3.7 0.0 copy-start.4
  3.7 0.7 %copy-done.4 = s32[2,3]{1,0:T(2,128)S(1)} copy-done((s32[2,3]{1,0:T(2,128)S(1)}, s32[2,3]{1,0:T(2,128)}, u32[]{:S(2)}) %copy-start.4) | copy-done | bytes 48
  4.3 33.8 %shard_map.55 = bf16[96,4096]{1,0:T(8,128)(2,1)S(1)} custom-call(s32[2,4]{1,0:T(2,128)S(1)} %copy-done.3, s32[2,3]{1,0:T(2,128)S(1)} %copy-done.4, bf16[384,1024]{1,0:T(8,128)(2,1)S(1)} %copy-done, bf16[384,256]{1,0:T(8,128)(2,1)S(1)} %copy-done.1, bf16[384,256]{1,0:T(8,128)(2,1)S(1)} %copy-done.2), custom_call_target="tpu_custom_call" | custom-call | tf_op jit(solution)/shard_map/pallas_call | solution.py:282
  38.2 0.9 %copy.7 = bf16[96,4096]{1,0:T(8,128)(2,1)} copy(bf16[96,4096]{1,0:T(8,128)(2,1)S(1)} %shard_map.55) | data formatting | bytes 1572864
Async XLA Ops:
  0.0 1.1 %copy-start = (bf16[384,1024]{1,0:T(8,128)(2,1)S(1)}, bf16[384,1024]{1,0:T(8,128)(2,1)}, u32[]{:S(2)}) copy-start(bf16[384,1024]{1,0:T(8,128)(2,1)} %q_ref.1) | copy-start | bytes 2359300
  1.1 0.9 %copy-start.1 = (bf16[384,256]{1,0:T(8,128)(2,1)S(1)}, bf16[384,256]{1,0:T(8,128)(2,1)}, u32[]{:S(2)}) copy-start(bf16[384,256]{1,0:T(8,128)(2,1)} %k_ref.1) | copy-start | bytes 589828
  2.1 0.9 %copy-start.2 = (bf16[384,256]{1,0:T(8,128)(2,1)S(1)}, bf16[384,256]{1,0:T(8,128)(2,1)}, u32[]{:S(2)}) copy-start(bf16[384,256]{1,0:T(8,128)(2,1)} %v_ref.1) | copy-start | bytes 589828
  3.0 0.7 %copy-start.3 = (s32[2,4]{1,0:T(2,128)S(1)}, s32[2,4]{1,0:T(2,128)}, u32[]{:S(2)}) copy-start(s32[2,4]{1,0:T(2,128)} %vert_ref.1) | copy-start | bytes 100
  3.7 0.7 %copy-start.4 = (s32[2,3]{1,0:T(2,128)S(1)}, s32[2,3]{1,0:T(2,128)}, u32[]{:S(2)}) copy-start(s32[2,3]{1,0:T(2,128)} %offs_ref.1) | copy-start | bytes 76

commit v2 on v1

--- a/solution.py
+++ b/solution.py
@@ -24,23 +24,31 @@
 def kernel(
     n_ctx,
     n_kvh,
+    vert_hbm,
+    offs_hbm,
+    q_hbm,
+    k_hbm,
+    v_hbm,
+    out_ref,
     vert_ref,
     offs_ref,
     q_ref,
     k_ref,
     v_ref,
-    out_ref,
     k_prev,
     v_prev,
     gath,
     obuf,
     kv_send,
     kv_recv,
-    vert_send,
-    vert_recv,
+    pair_send,
+    pair_recv,
+    chain_send,
+    chain_recv,
     out_send,
     out_recv,
     out_local,
+    load_sem,
 ):
     c = lax.axis_index("ctx")
     me = lax.axis_index("kvh")
@@ -55,16 +63,34 @@
     span = rows + tok
     per_shard = tok // BLK
 
-    def ctx_peer(i):
-        return lax.rem(c + 1 + i, n_ctx)
+    z, x = c // 2, c % 2
+    n_z = n_ctx // 2
+    partner = c + 1 - 2 * x
+
+    loads = [
+        pltpu.make_async_copy(src, dst, load_sem.at[i])
+        for i, (src, dst) in enumerate(
+            (
+                (vert_hbm, vert_ref),
+                (offs_hbm, offs_ref),
+                (k_hbm, k_ref),
+                (v_hbm, v_ref),
+                (q_hbm, q_ref),
+            )
+        )
+    ]
+    for load in loads:
+        load.start()
 
     barrier = pltpu.get_barrier_semaphore()
-    each(
-        n_ctx - 1,
-        lambda i: pl.semaphore_signal(
-            barrier, inc=1, device_id={"ctx": ctx_peer(i)}, device_id_type=MESH
-        ),
-    )
+    for step in (1, -1, 2, -2):
+
+        @pl.when((c + step >= 0) & (c + step < n_ctx))
+        def _():
+            pl.semaphore_signal(
+                barrier, inc=1, device_id={"ctx": c + step}, device_id_type=MESH
+            )
+
     for i in range(n_kvh - 1):
         pl.semaphore_signal(
             barrier,
@@ -72,6 +98,10 @@
             device_id={"kvh": lax.rem(me + 1 + i, n_kvh)},
             device_id_type=MESH,
         )
+    greeted = jnp.minimum(c, 2) + jnp.minimum(n_ctx - 1 - c, 2) + n_kvh - 1
+
+    for load in loads[:4]:
+        load.wait()
 
     for g in range(heads):
         row = jnp.int32(0)
@@ -84,32 +114,55 @@
         gath[c, g, 0] = k_ref[pl.ds(row, BLK), cols]
         gath[c, g, 1] = v_ref[pl.ds(row, BLK), cols]
 
-    pl.semaphore_wait(barrier, n_ctx - 1 + n_kvh - 1)
-
-    def vert_copy(i):
-        peer = ctx_peer(i)
+    pl.semaphore_wait(barrier, greeted)
+
+    pair_copy = pltpu.make_async_remote_copy(
+        src_ref=gath.at[c],
+        dst_ref=gath.at[c],
+        send_sem=pair_send,
+        recv_sem=pair_recv,
+        device_id={"ctx": partner},
+        device_id_type=MESH,
+    )
+
+    def chain_copy(pair, step):
+        part = gath.at[pl.ds(2 * pair, 2)]
         return pltpu.make_async_remote_copy(
-            src_ref=gath.at[c],
-            dst_ref=gath.at[c],
-            send_sem=vert_send.at[peer],
-            recv_sem=vert_recv.at[c],
-            device_id={"ctx": peer},
-            device_id_type=MESH,
-        )
-
-    def vert_arrival(i):
-        peer = ctx_peer(i)
-        return pltpu.make_async_remote_copy(
-            src_ref=gath.at[peer],
-            dst_ref=gath.at[peer],
-            send_sem=vert_send.at[peer],
-            recv_sem=vert_recv.at[peer],
-            device_id={"ctx": peer},
-            device_id_type=MESH,
-        )
+            src_ref=part,
+            dst_ref=part,
+            send_sem=chain_send.at[(step + 1) // 2, pair],
+            recv_sem=chain_recv.at[pair],
+            device_id={"ctx": c + 2 * step},
+            device_id_type=MESH,
+        )
+
+    def chain_round(i):
+        for step in (1, -1):
+            pair = z - step * i
+            there = (pair >= 0) & (pair < n_z)
+            onward = (z + step >= 0) & (z + step < n_z)
+            if not isinstance(i, int) or i > 0:
+
+                @pl.when(there)
+                def _():
+                    chain_copy(pair, step).wait_recv()
+
+            @pl.when(there & onward)
+            def _():
+                chain_copy(pair, step).start()
+
+    def chain_sent(i):
+        for step in (1, -1):
+            pair = z - step * i
+            there = (pair >= 0) & (pair < n_z)
+            onward = (z + step >= 0) & (z + step < n_z)
+
+            @pl.when(there & onward)
+            def _():
+                chain_copy(pair, step).wait_send()
 
     def kv_copy(which, chunk):
-        src, dst = ((k_ref, k_prev), (v_ref, v_prev))[which]
+        src, dst = ((k_hbm, k_prev), (v_hbm, v_prev))[which]
         part = pl.ds(chunk * rows, rows)
         return pltpu.make_async_remote_copy(
             src_ref=src.at[part],
@@ -120,13 +173,16 @@
             device_id_type=MESH,
         )
 
-    each(n_ctx - 1, lambda i: vert_copy(i).start())
+    pair_copy.start()
 
     @pl.when(c < n_ctx - 1)
     def _():
         for chunk in reversed(range(n_kvh)):
             for which in range(2):
                 kv_copy(which, chunk).start()
+
+    pair_copy.wait_recv()
+    chain_round(0)
 
     @pl.when(c == 0)
     def _():
@@ -150,7 +206,8 @@
             found = hit if found is None else found | hit
         return found
 
-    each(n_ctx - 1, lambda i: vert_arrival(i).wait_recv())
+    each(n_z - 1, lambda i: chain_round(i + 1))
+    loads[4].wait()
 
     vert_k, vert_v, vert_pos = [], [], []
     for g in range(heads):
@@ -250,7 +307,8 @@
             def _():
                 out_own(tile, g).start()
 
-    each(n_ctx - 1, lambda i: vert_copy(i).wait_send())
+    pair_copy.wait_send()
+    each(n_z, chain_sent)
 
     @pl.when(c < n_ctx - 1)
     def _():
@@ -276,29 +334,36 @@
     heads = vertical.shape[0]
     hd = keys.shape[1] // heads
     rows = tok // n_kvh
-    vmem = pl.BlockSpec(memory_space=pltpu.VMEM)
-    smem = pl.BlockSpec(memory_space=pltpu.SMEM)
+    hbm = pl.BlockSpec(memory_space=pltpu.HBM)
     dma = pltpu.SemaphoreType.DMA
     return pl.pallas_call(
         functools.partial(kernel, n_ctx, n_kvh),
         out_shape=jax.ShapeDtypeStruct((rows, queries.shape[1] * n_kvh), jnp.bfloat16),
-        in_specs=[smem, smem, vmem, vmem, vmem],
+        in_specs=[hbm] * 5,
         out_specs=pl.BlockSpec(memory_space=pl.ANY),
         scratch_shapes=[
+            pltpu.SMEM(vertical.shape, jnp.int32),
+            pltpu.SMEM(offsets.shape, jnp.int32),
+            pltpu.VMEM(queries.shape, jnp.bfloat16),
+            pltpu.VMEM(keys.shape, jnp.bfloat16),
+            pltpu.VMEM(values.shape, jnp.bfloat16),
             pltpu.VMEM(keys.shape, jnp.bfloat16),
             pltpu.VMEM(values.shape, jnp.bfloat16),
             pltpu.VMEM((n_ctx, heads, 2, BLK, hd), jnp.bfloat16),
             pltpu.VMEM(queries.shape, jnp.bfloat16),
             dma((2, n_kvh)),
             dma((2, n_kvh)),
-            dma((n_ctx,)),
-            dma((n_ctx,)),
+            dma,
+            dma,
+            dma((2, n_ctx // 2)),
+            dma((n_ctx // 2,)),
             dma((n_kvh, heads)),
             dma((n_kvh, heads)),
             dma((heads,)),
+            dma((5,)),
         ],
         compiler_params=pltpu.CompilerParams(
-            collective_id=0, has_side_effects=True, vmem_limit_bytes=48 * 1024 * 1024
+            collective_id=0, has_side_effects=True, vmem_limit_bytes=64 * 1024 * 1024
         ),
     )(vertical, offsets, queries, keys, values)
 

time: 39.3 us -> 44.5 us (1.13)
  the two profiles are of different devices: /device:TPU:16 before, /device:TPU:0 now
where the time goes in v2:
time: 44.5 us; the launch traced here: 44.3 us
  Pallas kernels  42.3 us (95%)
  local copies, waits for them, and re-layouts  2.06 us (5%)
    pallas_call x1, Pallas kernels, per_device(): pl.pallas_call(functools.partial(kernel, n_ctx, n_kvh), out_shape=jax.Sha...  42.3 us
    unnamed x1, local copies, waits for them, and re-layouts  2.06 us

profile of v2, /device:TPU:0, one launch (start us, length us, event | category | flops | bytes accessed | tf_op | source)
XLA Modules:
  0.0 44.3 jit_solution(16634321270358096994)
XLA Ops:
  0.0 42.3 %shard_map.55 = bf16[96,4096]{1,0:T(8,128)(2,1)} custom-call(s32[2,4]{1,0:T(2,128)} %vert_hbm.1, s32[2,3]{1,0:T(2,128)} %offs_hbm.1, bf16[384,1024]{1,0:T(8,128)(2,1)} %q_hbm.1, bf16[384,256]{1,0:T(8,128)(2,1)} %k_hbm.1, bf16[384,256]{1,0:T(8,128)(2,1)} %v_hbm.1), custom_call_target="tpu_custom_call" | custom-call | tf_op jit(solution)/shard_map/pallas_call | solution.py:339
  42.3 2.1 %copy.7 = bf16[96,4096]{1,0:T(8,128)(2,1)} copy(bf16[96,4096]{1,0:T(8,128)(2,1)} %shard_map.55) | data formatting | bytes 1572864

commit v3 on v2

--- a/solution.py
+++ b/solution.py
@@ -41,10 +41,10 @@
     obuf,
     kv_send,
     kv_recv,
-    pair_send,
-    pair_recv,
-    chain_send,
-    chain_recv,
+    col_send,
+    col_recv,
+    relay_send,
+    relay_recv,
     out_send,
     out_recv,
     out_local,
@@ -83,7 +83,17 @@
         load.start()
 
     barrier = pltpu.get_barrier_semaphore()
-    for step in (1, -1, 2, -2):
+
+    def column(i):
+        return lax.rem(z + 1 + i, n_z)
+
+    each(
+        n_z - 1,
+        lambda i: pl.semaphore_signal(
+            barrier, inc=1, device_id={"ctx": 2 * column(i) + x}, device_id_type=MESH
+        ),
+    )
+    for step in (1, -1):
 
         @pl.when((c + step >= 0) & (c + step < n_ctx))
         def _():
@@ -98,7 +108,7 @@
             device_id={"kvh": lax.rem(me + 1 + i, n_kvh)},
             device_id_type=MESH,
         )
-    greeted = jnp.minimum(c, 2) + jnp.minimum(n_ctx - 1 - c, 2) + n_kvh - 1
+    greeted = n_z - 1 + jnp.minimum(c, 1) + jnp.minimum(n_ctx - 1 - c, 1) + n_kvh - 1
 
     for load in loads[:4]:
         load.wait()
@@ -116,50 +126,53 @@
 
     pl.semaphore_wait(barrier, greeted)
 
-    pair_copy = pltpu.make_async_remote_copy(
-        src_ref=gath.at[c],
-        dst_ref=gath.at[c],
-        send_sem=pair_send,
-        recv_sem=pair_recv,
-        device_id={"ctx": partner},
-        device_id_type=MESH,
-    )
-
-    def chain_copy(pair, step):
-        part = gath.at[pl.ds(2 * pair, 2)]
+    def column_copy(i):
+        peer = column(i)
+        return pltpu.make_async_remote_copy(
+            src_ref=gath.at[c],
+            dst_ref=gath.at[c],
+            send_sem=col_send.at[peer],
+            recv_sem=col_recv.at[z],
+            device_id={"ctx": 2 * peer + x},
+            device_id_type=MESH,
+        )
+
+    def column_arrival(i):
+        peer = column(i)
+        return pltpu.make_async_remote_copy(
+            src_ref=gath.at[2 * peer + x],
+            dst_ref=gath.at[2 * peer + x],
+            send_sem=col_send.at[peer],
+            recv_sem=col_recv.at[peer],
+            device_id={"ctx": 2 * peer + x},
+            device_id_type=MESH,
+        )
+
+    def relay_copy(row):
+        part = gath.at[2 * row + x]
         return pltpu.make_async_remote_copy(
             src_ref=part,
             dst_ref=part,
-            send_sem=chain_send.at[(step + 1) // 2, pair],
-            recv_sem=chain_recv.at[pair],
-            device_id={"ctx": c + 2 * step},
-            device_id_type=MESH,
-        )
-
-    def chain_round(i):
-        for step in (1, -1):
-            pair = z - step * i
-            there = (pair >= 0) & (pair < n_z)
-            onward = (z + step >= 0) & (z + step < n_z)
-            if not isinstance(i, int) or i > 0:
-
-                @pl.when(there)
-                def _():
-                    chain_copy(pair, step).wait_recv()
-
-            @pl.when(there & onward)
-            def _():
-                chain_copy(pair, step).start()
-
-    def chain_sent(i):
-        for step in (1, -1):
-            pair = z - step * i
-            there = (pair >= 0) & (pair < n_z)
-            onward = (z + step >= 0) & (z + step < n_z)
-
-            @pl.when(there & onward)
-            def _():
-                chain_copy(pair, step).wait_send()
+            send_sem=relay_send.at[row],
+            recv_sem=relay_recv.at[row],
+            device_id={"ctx": partner},
+            device_id_type=MESH,
+        )
+
+    def relay_arrival(row):
+        part = gath.at[2 * row + 1 - x]
+        return pltpu.make_async_remote_copy(
+            src_ref=part,
+            dst_ref=part,
+            send_sem=relay_send.at[row],
+            recv_sem=relay_recv.at[row],
+            device_id={"ctx": partner},
+            device_id_type=MESH,
+        )
+
+    def relay_round(i):
+        column_arrival(i).wait_recv()
+        relay_copy(column(i)).start()
 
     def kv_copy(which, chunk):
         src, dst = ((k_hbm, k_prev), (v_hbm, v_prev))[which]
@@ -173,16 +186,18 @@
             device_id_type=MESH,
         )
 
-    pair_copy.start()
-
-    @pl.when(c < n_ctx - 1)
-    def _():
-        for chunk in reversed(range(n_kvh)):
-            for which in range(2):
-                kv_copy(which, chunk).start()
-
-    pair_copy.wait_recv()
-    chain_round(0)
+    def kv_start(chunks):
+        @pl.when(c < n_ctx - 1)
+        def _():
+            for chunk in chunks:
+                for which in range(2):
+                    kv_copy(which, chunk).start()
+
+    each(n_z - 1, lambda i: column_copy(i).start())
+    relay_copy(z).start()
+    kv_start(range(n_kvh - 1, n_kvh // 2 - 1, -1))
+    each(n_z - 1, relay_round)
+    kv_start(range(n_kvh // 2 - 1, -1, -1))
 
     @pl.when(c == 0)
     def _():
@@ -206,7 +221,7 @@
             found = hit if found is None else found | hit
         return found
 
-    each(n_z - 1, lambda i: chain_round(i + 1))
+    each(n_z, lambda i: relay_arrival(i).wait_recv())
     loads[4].wait()
 
     vert_k, vert_v, vert_pos = [], [], []
@@ -307,8 +322,8 @@
             def _():
                 out_own(tile, g).start()
 
-    pair_copy.wait_send()
-    each(n_z, chain_sent)
+    each(n_z - 1, lambda i: column_copy(i).wait_send())
+    each(n_z, lambda i: relay_copy(i).wait_send())
 
     @pl.when(c < n_ctx - 1)
     def _():
@@ -340,7 +355,7 @@
         functools.partial(kernel, n_ctx, n_kvh),
         out_shape=jax.ShapeDtypeStruct((rows, queries.shape[1] * n_kvh), jnp.bfloat16),
         in_specs=[hbm] * 5,
-        out_specs=pl.BlockSpec(memory_space=pl.ANY),
+        out_specs=pl.BlockSpec(memory_space=pltpu.VMEM),
         scratch_shapes=[
             pltpu.SMEM(vertical.shape, jnp.int32),
             pltpu.SMEM(offsets.shape, jnp.int32),
@@ -353,9 +368,9 @@
             pltpu.VMEM(queries.shape, jnp.bfloat16),
             dma((2, n_kvh)),
             dma((2, n_kvh)),
-            dma,
-            dma,
-            dma((2, n_ctx // 2)),
+            dma((n_ctx // 2,)),
+            dma((n_ctx // 2,)),
+            dma((n_ctx // 2,)),
             dma((n_ctx // 2,)),
             dma((n_kvh, heads)),
             dma((n_kvh, heads)),

time: 44.5 us -> 42 us (0.944)
  the two profiles are of different devices: /device:TPU:0 before, /device:TPU:8 now
where the time goes in v3:
time: 42 us; the launch traced here: 41.8 us
  Pallas kernels  39.7 us (95%)
  local copies, waits for them, and re-layouts  2.06 us (5%)
    pallas_call x1, Pallas kernels, per_device(): pl.pallas_call(functools.partial(kernel, n_ctx, n_kvh), out_shape=jax.Sha...  39.7 us
    unnamed x1, local copies, waits for them, and re-layouts  2.06 us

profile of v3, /device:TPU:8, one launch (start us, length us, event | category | flops | bytes accessed | tf_op | source)
XLA Modules:
  0.0 41.8 jit_solution(5568865192679760401)
XLA Ops:
  0.0 39.7 %shard_map.55 = bf16[96,4096]{1,0:T(8,128)(2,1)} custom-call(s32[2,4]{1,0:T(2,128)} %vert_hbm.1, s32[2,3]{1,0:T(2,128)} %offs_hbm.1, bf16[384,1024]{1,0:T(8,128)(2,1)} %q_hbm.1, bf16[384,256]{1,0:T(8,128)(2,1)} %k_hbm.1, bf16[384,256]{1,0:T(8,128)(2,1)} %v_hbm.1), custom_call_target="tpu_custom_call" | custom-call | tf_op jit(solution)/shard_map/pallas_call | solution.py:354
  39.7 2.1 %copy.7 = bf16[96,4096]{1,0:T(8,128)(2,1)} copy(bf16[96,4096]{1,0:T(8,128)(2,1)} %shard_map.55) | data formatting | bytes 1572864

commit v4 on v1

--- a/solution.py
+++ b/solution.py
@@ -24,12 +24,17 @@
 def kernel(
     n_ctx,
     n_kvh,
+    vert_hbm,
+    offs_hbm,
+    q_hbm,
+    k_hbm,
+    v_hbm,
+    out_ref,
     vert_ref,
     offs_ref,
     q_ref,
     k_ref,
     v_ref,
-    out_ref,
     k_prev,
     v_prev,
     gath,
@@ -41,6 +46,8 @@
     out_send,
     out_recv,
     out_local,
+    load_sem,
+    band_bias,
 ):
     c = lax.axis_index("ctx")
     me = lax.axis_index("kvh")
@@ -58,6 +65,21 @@
     def ctx_peer(i):
         return lax.rem(c + 1 + i, n_ctx)
 
+    loads = [
+        pltpu.make_async_copy(src, dst, load_sem.at[i])
+        for i, (src, dst) in enumerate(
+            (
+                (vert_hbm, vert_ref),
+                (offs_hbm, offs_ref),
+                (k_hbm, k_ref),
+                (v_hbm, v_ref),
+                (q_hbm, q_ref),
+            )
+        )
+    ]
+    for load in loads:
+        load.start()
+
     barrier = pltpu.get_barrier_semaphore()
     each(
         n_ctx - 1,
@@ -73,6 +95,9 @@
             device_id_type=MESH,
         )
 
+    for load in loads[:4]:
+        load.wait()
+
     for g in range(heads):
         row = jnp.int32(0)
         for j in range(slots):
@@ -109,7 +134,7 @@
         )
 
     def kv_copy(which, chunk):
-        src, dst = ((k_ref, k_prev), (v_ref, v_prev))[which]
+        src, dst = ((k_hbm, k_prev), (v_hbm, v_prev))[which]
         part = pl.ds(chunk * rows, rows)
         return pltpu.make_async_remote_copy(
             src_ref=src.at[part],
@@ -149,6 +174,10 @@
             hit = (gap >= 0) & (gap < BLK)
             found = hit if found is None else found | hit
         return found
+
+    for g in range(heads):
+        band_bias[g] = jnp.where(in_bands(lag, g), 0.0, NEG)
+    loads[4].wait()
 
     each(n_ctx - 1, lambda i: vert_arrival(i).wait_recv())
 
@@ -218,10 +247,10 @@
             dims = (((1,), (1,)), ((), ()))
             score_w = lax.dot_general(q, keys, dims, preferred_element_type=jnp.float32)
             score_v = lax.dot_general(q, vert_k[g], dims, preferred_element_type=jnp.float32)
-            mask_w = in_bands(lag, g) & (window_col >= before)
+            bias_w = jnp.where(window_col >= before, band_bias[g], NEG)
             vert_lag = vert_row + (c * tok + base) - vert_pos[g]
             mask_v = (vert_lag >= 0) & ~in_bands(vert_lag, g)
-            score_w = jnp.where(mask_w[None], score_w.reshape(group, rows, span), NEG)
+            score_w = score_w.reshape(group, rows, span) + bias_w[None]
             score_v = jnp.where(mask_v[None], score_v.reshape(group, rows, slots * BLK), NEG)
             top = jnp.maximum(
                 jnp.max(score_w, axis=-1, keepdims=True), jnp.max(score_v, axis=-1, keepdims=True)
@@ -276,15 +305,19 @@
     heads = vertical.shape[0]
     hd = keys.shape[1] // heads
     rows = tok // n_kvh
-    vmem = pl.BlockSpec(memory_space=pltpu.VMEM)
-    smem = pl.BlockSpec(memory_space=pltpu.SMEM)
+    hbm = pl.BlockSpec(memory_space=pltpu.HBM)
     dma = pltpu.SemaphoreType.DMA
     return pl.pallas_call(
         functools.partial(kernel, n_ctx, n_kvh),
         out_shape=jax.ShapeDtypeStruct((rows, queries.shape[1] * n_kvh), jnp.bfloat16),
-        in_specs=[smem, smem, vmem, vmem, vmem],
-        out_specs=pl.BlockSpec(memory_space=pl.ANY),
+        in_specs=[hbm] * 5,
+        out_specs=pl.BlockSpec(memory_space=pltpu.VMEM),
         scratch_shapes=[
+            pltpu.SMEM(vertical.shape, jnp.int32),
+            pltpu.SMEM(offsets.shape, jnp.int32),
+            pltpu.VMEM(queries.shape, jnp.bfloat16),
+            pltpu.VMEM(keys.shape, jnp.bfloat16),
+            pltpu.VMEM(values.shape, jnp.bfloat16),
             pltpu.VMEM(keys.shape, jnp.bfloat16),
             pltpu.VMEM(values.shape, jnp.bfloat16),
             pltpu.VMEM((n_ctx, heads, 2, BLK, hd), jnp.bfloat16),
@@ -296,9 +329,11 @@
             dma((n_kvh, heads)),
             dma((n_kvh, heads)),
             dma((heads,)),
+            dma((5,)),
+            pltpu.VMEM((heads, rows, rows + tok), jnp.float32),
         ],
         compiler_params=pltpu.CompilerParams(
-            collective_id=0, has_side_effects=True, vmem_limit_bytes=48 * 1024 * 1024
+            collective_id=0, has_side_effects=True, vmem_limit_bytes=64 * 1024 * 1024
         ),
     )(vertical, offsets, queries, keys, values)
 

time: 39.3 us -> 36.3 us (0.924)
  local copies, waits for them, and re-layouts: 5.22 us -> 2.06 us
    unnamed x11 -> x1, local copies, waits for them, and re-layouts: 5.22 us -> 2.06 us
where the time goes in v4:
time: 36.3 us; the launch traced here: 36.1 us
  Pallas kernels  34 us (94%)
  local copies, waits for them, and re-layouts  2.06 us (6%)
    pallas_call x1, Pallas kernels, per_device(): pl.pallas_call(functools.partial(kernel, n_ctx, n_kvh), out_shape=jax.Sha...  34 us
    unnamed x1, local copies, waits for them, and re-layouts  2.06 us

profile of v4, /device:TPU:16, one launch (start us, length us, event | category | flops | bytes accessed | tf_op | source)
XLA Modules:
  0.0 36.1 jit_solution(13268279747664802034)
XLA Ops:
  0.0 34.0 %shard_map.55 = bf16[96,4096]{1,0:T(8,128)(2,1)} custom-call(s32[2,4]{1,0:T(2,128)} %vert_hbm.1, s32[2,3]{1,0:T(2,128)} %offs_hbm.1, bf16[384,1024]{1,0:T(8,128)(2,1)} %q_hbm.1, bf16[384,256]{1,0:T(8,128)(2,1)} %k_hbm.1, bf16[384,256]{1,0:T(8,128)(2,1)} %v_hbm.1), custom_call_target="tpu_custom_call" | custom-call | tf_op jit(solution)/shard_map/pallas_call | solution.py:310
  34.0 2.1 %copy.7 = bf16[96,4096]{1,0:T(8,128)(2,1)} copy(bf16[96,4096]{1,0:T(8,128)(2,1)} %shard_map.55) | data formatting | bytes 1572864

commit v5 on v4

--- a/solution.py
+++ b/solution.py
@@ -48,6 +48,9 @@
     out_local,
     load_sem,
     band_bias,
+    relay,
+    relay_send,
+    relay_recv,
 ):
     c = lax.axis_index("ctx")
     me = lax.axis_index("kvh")
@@ -133,8 +136,11 @@
             device_id_type=MESH,
         )
 
+    x = c % 2
+    sides = ((k_hbm, k_prev), (v_hbm, v_prev))
+
     def kv_copy(which, chunk):
-        src, dst = ((k_hbm, k_prev), (v_hbm, v_prev))[which]
+        src, dst = sides[which]
         part = pl.ds(chunk * rows, rows)
         return pltpu.make_async_remote_copy(
             src_ref=src.at[part],
@@ -145,13 +151,42 @@
             device_id_type=MESH,
         )
 
+    def odd_copy(which, chunk):
+        part = pl.ds(chunk * rows, rows)
+        return pltpu.make_async_remote_copy(
+            src_ref=sides[which][0].at[part],
+            dst_ref=relay.at[part],
+            send_sem=kv_send.at[which, chunk],
+            recv_sem=relay_recv.at[chunk],
+            device_id={"ctx": (c - 1, c + 2)[which]},
+            device_id_type=MESH,
+        )
+
+    def onward_copy(which, chunk):
+        part = pl.ds(chunk * rows, rows)
+        return pltpu.make_async_remote_copy(
+            src_ref=relay.at[part],
+            dst_ref=sides[which][1].at[part],
+            send_sem=relay_send.at[chunk],
+            recv_sem=kv_recv.at[which, chunk],
+            device_id={"ctx": (c + 2, c - 1)[which]},
+            device_id_type=MESH,
+        )
+
+    odd_sends = (x == 1) & (c < n_ctx - 1)
+    relays = ((x == 0) & (c < n_ctx - 2), (x == 1) & (c > 1))
+
     each(n_ctx - 1, lambda i: vert_copy(i).start())
-
-    @pl.when(c < n_ctx - 1)
-    def _():
-        for chunk in reversed(range(n_kvh)):
-            for which in range(2):
+    for chunk in reversed(range(n_kvh)):
+        for which in range(2):
+
+            @pl.when(x == 0)
+            def _():
                 kv_copy(which, chunk).start()
+
+            @pl.when(odd_sends)
+            def _():
+                odd_copy(which, chunk).start()
 
     @pl.when(c == 0)
     def _():
@@ -178,6 +213,14 @@
     for g in range(heads):
         band_bias[g] = jnp.where(in_bands(lag, g), 0.0, NEG)
     loads[4].wait()
+
+    for which in range(2):
+
+        @pl.when(relays[which])
+        def _():
+            for chunk in reversed(range(n_kvh)):
+                odd_copy(which, chunk).wait_recv()
+                onward_copy(which, chunk).start()
 
     each(n_ctx - 1, lambda i: vert_arrival(i).wait_recv())
 
@@ -281,11 +324,16 @@
 
     each(n_ctx - 1, lambda i: vert_copy(i).wait_send())
 
-    @pl.when(c < n_ctx - 1)
-    def _():
-        for chunk in range(n_kvh):
-            for which in range(2):
+    for chunk in range(n_kvh):
+        for which in range(2):
+
+            @pl.when((x == 0) | odd_sends)
+            def _():
                 kv_copy(which, chunk).wait_send()
+
+            @pl.when(relays[which])
+            def _():
+                onward_copy(which, chunk).wait_send()
 
     for peer in range(n_kvh):
         for g in range(heads):
@@ -331,6 +379,9 @@
             dma((heads,)),
             dma((5,)),
             pltpu.VMEM((heads, rows, rows + tok), jnp.float32),
+            pltpu.VMEM(keys.shape, jnp.bfloat16),
+            dma((n_kvh,)),
+            dma((n_kvh,)),
         ],
         compiler_params=pltpu.CompilerParams(
             collective_id=0, has_side_effects=True, vmem_limit_bytes=64 * 1024 * 1024

time: 36.3 us -> 37.2 us (1.025)
  Pallas kernels: 34 us -> 34.7 us
    pallas_call x1, Pallas kernels: 34 us -> 34.7 us  [per_device(): pl.pallas_call(functools.partial(kernel, n_ctx, n_kvh), out_shape=jax.Sha...]
where the time goes in v5:
time: 37.2 us; the launch traced here: 36.8 us
  Pallas kernels  34.7 us (93%)
  local copies, waits for them, and re-layouts  2.06 us (6%)
    pallas_call x1, Pallas kernels, per_device(): pl.pallas_call(functools.partial(kernel, n_ctx, n_kvh), out_shape=jax.Sha...  34.7 us
    unnamed x1, local copies, waits for them, and re-layouts  2.06 us

profile of v5, /device:TPU:16, one launch (start us, length us, event | category | flops | bytes accessed | tf_op | source)
XLA Modules:
  0.0 36.8 jit_solution(3024300014734921318)
XLA Ops:
  0.0 34.7 %shard_map.55 = bf16[96,4096]{1,0:T(8,128)(2,1)} custom-call(s32[2,4]{1,0:T(2,128)} %vert_hbm.1, s32[2,3]{1,0:T(2,128)} %offs_hbm.1, bf16[384,1024]{1,0:T(8,128)(2,1)} %q_hbm.1, bf16[384,256]{1,0:T(8,128)(2,1)} %k_hbm.1, bf16[384,256]{1,0:T(8,128)(2,1)} %v_hbm.1), custom_call_target="tpu_custom_call" | custom-call | tf_op jit(solution)/shard_map/pallas_call | solution.py:358
  34.7 2.1 %copy.7 = bf16[96,4096]{1,0:T(8,128)(2,1)} copy(bf16[96,4096]{1,0:T(8,128)(2,1)} %shard_map.55) | data formatting | bytes 1572864

commit v6 on v4

--- a/solution.py
+++ b/solution.py
@@ -48,6 +48,9 @@
     out_local,
     load_sem,
     band_bias,
+    win_top,
+    win_total,
+    win_out,
 ):
     c = lax.axis_index("ctx")
     me = lax.axis_index("kvh")
@@ -145,13 +148,13 @@
             device_id_type=MESH,
         )
 
-    each(n_ctx - 1, lambda i: vert_copy(i).start())
-
     @pl.when(c < n_ctx - 1)
     def _():
         for chunk in reversed(range(n_kvh)):
             for which in range(2):
                 kv_copy(which, chunk).start()
+
+    each(n_ctx - 1, lambda i: vert_copy(i).start())
 
     @pl.when(c == 0)
     def _():
@@ -178,6 +181,74 @@
     for g in range(heads):
         band_bias[g] = jnp.where(in_bands(lag, g), 0.0, NEG)
     loads[4].wait()
+
+    factor = math.log2(math.e) * hd**-0.5
+
+    def out_copy(tile, g):
+        return pltpu.make_async_remote_copy(
+            src_ref=obuf.at[pl.ds(tile * rows, rows), pl.ds(g * gcols, gcols)],
+            dst_ref=out_ref.at[
+                :, pl.ds(pl.multiple_of(me * heads * gcols + g * gcols, gcols), gcols)
+            ],
+            send_sem=out_send.at[tile, g],
+            recv_sem=out_recv.at[me, g],
+            device_id={"kvh": tile},
+            device_id_type=MESH,
+        )
+
+    def out_own(tile, g):
+        return pltpu.make_async_copy(
+            obuf.at[pl.ds(tile * rows, rows), pl.ds(g * gcols, gcols)],
+            out_ref.at[
+                :, pl.ds(pl.multiple_of(me * heads * gcols + g * gcols, gcols), gcols)
+            ],
+            out_local.at[g],
+        )
+
+    def out_arrival(peer, g):
+        return pltpu.make_async_remote_copy(
+            src_ref=obuf.at[pl.ds(0, rows), pl.ds(g * gcols, gcols)],
+            dst_ref=out_ref.at[:, pl.ds(peer * heads * gcols + g * gcols, gcols)],
+            send_sem=out_send.at[peer, g],
+            recv_sem=out_recv.at[peer, g],
+            device_id={"kvh": peer},
+            device_id_type=MESH,
+        )
+
+    dims = (((1,), (1,)), ((), ()))
+
+    for tile in reversed(range(n_kvh)):
+        base = tile * rows
+
+        @pl.when(c > 0)
+        def _():
+            for which in range(2):
+                kv_copy(which, tile).wait_recv()
+
+        before = jnp.where(c == 0, tok - base, 0)
+        for g in range(heads):
+            cols = slice(g * hd, (g + 1) * hd)
+            q = jnp.concatenate(
+                [
+                    q_ref[base : base + rows, (g * group + h) * hd : (g * group + h + 1) * hd]
+                    for h in range(group)
+                ],
+                axis=0,
+            )
+            keys = jnp.concatenate([k_prev[base:, cols], k_ref[: base + rows, cols]], axis=0)
+            vals = jnp.concatenate([v_prev[base:, cols], v_ref[: base + rows, cols]], axis=0)
+            score = lax.dot_general(q, keys, dims, preferred_element_type=jnp.float32)
+            bias = jnp.where(window_col >= before, band_bias[g], NEG)
+            score = score.reshape(group, rows, span) + bias[None]
+            top = jnp.max(score, axis=-1, keepdims=True)
+            weight = jnp.exp2((score - top) * factor)
+            win_top[tile, g] = top.reshape(group * rows, 1)
+            win_total[tile, g] = jnp.sum(weight, axis=-1, keepdims=True).reshape(group * rows, 1)
+            win_out[tile, g] = jnp.dot(
+                weight.astype(jnp.bfloat16).reshape(group * rows, span),
+                vals,
+                preferred_element_type=jnp.float32,
+            )
 
     each(n_ctx - 1, lambda i: vert_arrival(i).wait_recv())
 
@@ -191,85 +262,36 @@
             first = jnp.where(vert_lane // BLK == j, vert_ref[g, j], first)
         vert_pos.append(first * BLK + vert_lane % BLK)
 
-    factor = math.log2(math.e) * hd**-0.5
-
-    def out_copy(tile, g):
-        return pltpu.make_async_remote_copy(
-            src_ref=obuf.at[pl.ds(tile * rows, rows), pl.ds(g * gcols, gcols)],
-            dst_ref=out_ref.at[
-                :, pl.ds(pl.multiple_of(me * heads * gcols + g * gcols, gcols), gcols)
-            ],
-            send_sem=out_send.at[tile, g],
-            recv_sem=out_recv.at[me, g],
-            device_id={"kvh": tile},
-            device_id_type=MESH,
-        )
-
-    def out_own(tile, g):
-        return pltpu.make_async_copy(
-            obuf.at[pl.ds(tile * rows, rows), pl.ds(g * gcols, gcols)],
-            out_ref.at[
-                :, pl.ds(pl.multiple_of(me * heads * gcols + g * gcols, gcols), gcols)
-            ],
-            out_local.at[g],
-        )
-
-    def out_arrival(peer, g):
-        return pltpu.make_async_remote_copy(
-            src_ref=obuf.at[pl.ds(0, rows), pl.ds(g * gcols, gcols)],
-            dst_ref=out_ref.at[:, pl.ds(peer * heads * gcols + g * gcols, gcols)],
-            send_sem=out_send.at[peer, g],
-            recv_sem=out_recv.at[peer, g],
-            device_id={"kvh": peer},
-            device_id_type=MESH,
-        )
-
-    for tile in reversed(range(n_kvh)):
-        base = tile * rows
-
-        @pl.when(c > 0)
-        def _():
-            for which in range(2):
-                kv_copy(which, tile).wait_recv()
-
-        before = jnp.where(c == 0, tok - base, 0)
+    half = n_kvh // 2
+    for turn in range(n_kvh):
+        tile = lax.rem(half * (1 - me // half) + turn, n_kvh)
+        base = pl.multiple_of(tile * rows, rows)
         for g in range(heads):
-            cols = slice(g * hd, (g + 1) * hd)
             q = jnp.concatenate(
                 [
-                    q_ref[base : base + rows, (g * group + h) * hd : (g * group + h + 1) * hd]
+                    q_ref[pl.ds(base, rows), (g * group + h) * hd : (g * group + h + 1) * hd]
                     for h in range(group)
                 ],
                 axis=0,
             )
-            keys = jnp.concatenate([k_prev[base:, cols], k_ref[: base + rows, cols]], axis=0)
-            vals = jnp.concatenate([v_prev[base:, cols], v_ref[: base + rows, cols]], axis=0)
-            dims = (((1,), (1,)), ((), ()))
-            score_w = lax.dot_general(q, keys, dims, preferred_element_type=jnp.float32)
-            score_v = lax.dot_general(q, vert_k[g], dims, preferred_element_type=jnp.float32)
-            bias_w = jnp.where(window_col >= before, band_bias[g], NEG)
+            score = lax.dot_general(q, vert_k[g], dims, preferred_element_type=jnp.float32)
             vert_lag = vert_row + (c * tok + base) - vert_pos[g]
-            mask_v = (vert_lag >= 0) & ~in_bands(vert_lag, g)
-            score_w = score_w.reshape(group, rows, span) + bias_w[None]
-            score_v = jnp.where(mask_v[None], score_v.reshape(group, rows, slots * BLK), NEG)
-            top = jnp.maximum(
-                jnp.max(score_w, axis=-1, keepdims=True), jnp.max(score_v, axis=-1, keepdims=True)
-            )
-            exp_w = jnp.exp2((score_w - top) * factor)
-            exp_v = jnp.exp2((score_v - top) * factor)
-            total = jnp.sum(exp_w, axis=-1, keepdims=True) + jnp.sum(exp_v, axis=-1, keepdims=True)
-            blended = jnp.dot(
-                exp_w.astype(jnp.bfloat16).reshape(group * rows, span),
-                vals,
-                preferred_element_type=jnp.float32,
-            ) + jnp.dot(
-                exp_v.astype(jnp.bfloat16).reshape(group * rows, slots * BLK),
-                vert_v[g],
-                preferred_element_type=jnp.float32,
-            )
-            result = (blended.reshape(group, rows, hd) / total).astype(jnp.bfloat16)
+            mask = (vert_lag >= 0) & ~in_bands(vert_lag, g)
+            score = jnp.where(mask[None], score.reshape(group, rows, slots * BLK), NEG)
+            score = score.reshape(group * rows, slots * BLK)
+            before_top = win_top[tile, g]
+            top = jnp.maximum(before_top, jnp.max(score, axis=-1, keepdims=True))
+            weight = jnp.exp2((score - top) * factor)
+            fade = jnp.exp2((before_top - top) * factor)
+            total = win_total[tile, g] * fade + jnp.sum(weight, axis=-1, keepdims=True)
+            blended = win_out[tile, g] * fade + jnp.dot(
+                weight.astype(jnp.bfloat16), vert_v[g], preferred_element_type=jnp.float32
+            )
+            result = (blended / total).astype(jnp.bfloat16)
             for h in range(group):
-                obuf[base : base + rows, (g * group + h) * hd : (g * group + h + 1) * hd] = result[h]
+                obuf[pl.ds(base, rows), (g * group + h) * hd : (g * group + h + 1) * hd] = result[
+                    h * rows : (h + 1) * rows
+                ]
 
             @pl.when(tile != me)
             def _():
@@ -305,6 +327,7 @@
     heads = vertical.shape[0]
     hd = keys.shape[1] // heads
     rows = tok // n_kvh
+    group = queries.shape[1] // keys.shape[1]
     hbm = pl.BlockSpec(memory_space=pltpu.HBM)
     dma = pltpu.SemaphoreType.DMA
     return pl.pallas_call(
@@ -331,6 +354,9 @@
             dma((heads,)),
             dma((5,)),
             pltpu.VMEM((heads, rows, rows + tok), jnp.float32),
+            pltpu.VMEM((n_kvh, heads, group * rows, 1), jnp.float32),
+            pltpu.VMEM((n_kvh, heads, group * rows, 1), jnp.float32),
+            pltpu.VMEM((n_kvh, heads, group * rows, hd), jnp.float32),
         ],
         compiler_params=pltpu.CompilerParams(
             collective_id=0, has_side_effects=True, vmem_limit_bytes=64 * 1024 * 1024

time: 36.3 us -> 38.4 us (1.058)
  the two profiles are of different devices: /device:TPU:16 before, /device:TPU:27 now
where the time goes in v6:
time: 38.4 us; the launch traced here: 38.2 us
  Pallas kernels  36.1 us (94%)
  local copies, waits for them, and re-layouts  2.06 us (5%)
    pallas_call x1, Pallas kernels, per_device(): pl.pallas_call(functools.partial(kernel, n_ctx, n_kvh), out_shape=jax.Sha...  36.1 us
    unnamed x1, local copies, waits for them, and re-layouts  2.06 us

profile of v6, /device:TPU:27, one launch (start us, length us, event | category | flops | bytes accessed | tf_op | source)
XLA Modules:
  0.0 38.2 jit_solution(6543445685187249758)
XLA Ops:
  0.0 36.1 %shard_map.55 = bf16[96,4096]{1,0:T(8,128)(2,1)} custom-call(s32[2,4]{1,0:T(2,128)} %vert_hbm.1, s32[2,3]{1,0:T(2,128)} %offs_hbm.1, bf16[384,1024]{1,0:T(8,128)(2,1)} %q_hbm.1, bf16[384,256]{1,0:T(8,128)(2,1)} %k_hbm.1, bf16[384,256]{1,0:T(8,128)(2,1)} %v_hbm.1), custom_call_target="tpu_custom_call" | custom-call | tf_op jit(solution)/shard_map/pallas_call | solution.py:333
  36.1 2.1 %copy.7 = bf16[96,4096]{1,0:T(8,128)(2,1)} copy(bf16[96,4096]{1,0:T(8,128)(2,1)} %shard_map.55) | data formatting | bytes 1572864

commit v7 on v6

--- a/solution.py
+++ b/solution.py
@@ -41,8 +41,10 @@
     obuf,
     kv_send,
     kv_recv,
-    vert_send,
-    vert_recv,
+    col_send,
+    col_recv,
+    vrelay_send,
+    vrelay_recv,
     out_send,
     out_recv,
     out_local,
@@ -51,6 +53,9 @@
     win_top,
     win_total,
     win_out,
+    relay,
+    relay_send,
+    relay_recv,
 ):
     c = lax.axis_index("ctx")
     me = lax.axis_index("kvh")
@@ -65,6 +70,13 @@
     span = rows + tok
     per_shard = tok // BLK
 
+    z, x = c // 2, c % 2
+    n_z = n_ctx // 2
+    partner = c + 1 - 2 * x
+
+    def column(i):
+        return lax.rem(z + 1 + i, n_z)
+
     def ctx_peer(i):
         return lax.rem(c + 1 + i, n_ctx)
 
@@ -114,30 +126,58 @@
 
     pl.semaphore_wait(barrier, n_ctx - 1 + n_kvh - 1)
 
-    def vert_copy(i):
-        peer = ctx_peer(i)
+    def column_copy(i):
+        peer = column(i)
         return pltpu.make_async_remote_copy(
             src_ref=gath.at[c],
             dst_ref=gath.at[c],
-            send_sem=vert_send.at[peer],
-            recv_sem=vert_recv.at[c],
-            device_id={"ctx": peer},
-            device_id_type=MESH,
-        )
-
-    def vert_arrival(i):
-        peer = ctx_peer(i)
-        return pltpu.make_async_remote_copy(
-            src_ref=gath.at[peer],
-            dst_ref=gath.at[peer],
-            send_sem=vert_send.at[peer],
-            recv_sem=vert_recv.at[peer],
-            device_id={"ctx": peer},
-            device_id_type=MESH,
-        )
+            send_sem=col_send.at[peer],
+            recv_sem=col_recv.at[z],
+            device_id={"ctx": 2 * peer + x},
+            device_id_type=MESH,
+        )
+
+    def column_arrival(i):
+        peer = column(i)
+        return pltpu.make_async_remote_copy(
+            src_ref=gath.at[2 * peer + x],
+            dst_ref=gath.at[2 * peer + x],
+            send_sem=col_send.at[peer],
+            recv_sem=col_recv.at[peer],
+            device_id={"ctx": 2 * peer + x},
+            device_id_type=MESH,
+        )
+
+    def relay_copy(row):
+        part = gath.at[2 * row + x]
+        return pltpu.make_async_remote_copy(
+            src_ref=part,
+            dst_ref=part,
+            send_sem=vrelay_send.at[row],
+            recv_sem=vrelay_recv.at[row],
+            device_id={"ctx": partner},
+            device_id_type=MESH,
+        )
+
+    def relay_arrival(row):
+        part = gath.at[2 * row + 1 - x]
+        return pltpu.make_async_remote_copy(
+            src_ref=part,
+            dst_ref=part,
+            send_sem=vrelay_send.at[row],
+            recv_sem=vrelay_recv.at[row],
+            device_id={"ctx": partner},
+            device_id_type=MESH,
+        )
+
+    def relay_round(i):
+        column_arrival(i).wait_recv()
+        relay_copy(column(i)).start()
+
+    sides = ((k_hbm, k_prev), (v_hbm, v_prev))
 
     def kv_copy(which, chunk):
-        src, dst = ((k_hbm, k_prev), (v_hbm, v_prev))[which]
+        src, dst = sides[which]
         part = pl.ds(chunk * rows, rows)
         return pltpu.make_async_remote_copy(
             src_ref=src.at[part],
@@ -148,13 +188,43 @@
             device_id_type=MESH,
         )
 
-    @pl.when(c < n_ctx - 1)
-    def _():
-        for chunk in reversed(range(n_kvh)):
-            for which in range(2):
+    def odd_copy(which, chunk):
+        part = pl.ds(chunk * rows, rows)
+        return pltpu.make_async_remote_copy(
+            src_ref=sides[which][0].at[part],
+            dst_ref=relay.at[part],
+            send_sem=kv_send.at[which, chunk],
+            recv_sem=relay_recv.at[chunk],
+            device_id={"ctx": (c - 1, c + 2)[which]},
+            device_id_type=MESH,
+        )
+
+    def onward_copy(which, chunk):
+        part = pl.ds(chunk * rows, rows)
+        return pltpu.make_async_remote_copy(
+            src_ref=relay.at[part],
+            dst_ref=sides[which][1].at[part],
+            send_sem=relay_send.at[chunk],
+            recv_sem=kv_recv.at[which, chunk],
+            device_id={"ctx": (c + 2, c - 1)[which]},
+            device_id_type=MESH,
+        )
+
+    odd_sends = (x == 1) & (c < n_ctx - 1)
+    relays = ((x == 0) & (c < n_ctx - 2), (x == 1) & (c > 1))
+
+    each(n_z - 1, lambda i: column_copy(i).start())
+    relay_copy(z).start()
+    for chunk in reversed(range(n_kvh)):
+        for which in range(2):
+
+            @pl.when(x == 0)
+            def _():
                 kv_copy(which, chunk).start()
 
-    each(n_ctx - 1, lambda i: vert_copy(i).start())
+            @pl.when(odd_sends)
+            def _():
+                odd_copy(which, chunk).start()
 
     @pl.when(c == 0)
     def _():
@@ -219,6 +289,15 @@
 
     for tile in reversed(range(n_kvh)):
         base = tile * rows
+        for which in range(2):
+
+            @pl.when(relays[which])
+            def _():
+                odd_copy(which, tile).wait_recv()
+                onward_copy(which, tile).start()
+
+        if tile == n_kvh - 2:
+            each(n_z - 1, relay_round)
 
         @pl.when(c > 0)
         def _():
@@ -250,7 +329,7 @@
                 preferred_element_type=jnp.float32,
             )
 
-    each(n_ctx - 1, lambda i: vert_arrival(i).wait_recv())
+    each(n_z, lambda i: relay_arrival(i).wait_recv())
 
     vert_k, vert_v, vert_pos = [], [], []
     for g in range(heads):
@@ -301,13 +380,18 @@
             def _():
                 out_own(tile, g).start()
 
-    each(n_ctx - 1, lambda i: vert_copy(i).wait_send())
-
-    @pl.when(c < n_ctx - 1)
-    def _():
-        for chunk in range(n_kvh):
-            for which in range(2):
+    each(n_z - 1, lambda i: column_copy(i).wait_send())
+    each(n_z, lambda i: relay_copy(i).wait_send())
+    for chunk in range(n_kvh):
+        for which in range(2):
+
+            @pl.when((x == 0) | odd_sends)
+            def _():
                 kv_copy(which, chunk).wait_send()
+
+            @pl.when(relays[which])
+            def _():
+                onward_copy(which, chunk).wait_send()
 
     for peer in range(n_kvh):
         for g in range(heads):
@@ -347,8 +431,10 @@
             pltpu.VMEM(queries.shape, jnp.bfloat16),
             dma((2, n_kvh)),
             dma((2, n_kvh)),
-            dma((n_ctx,)),
-            dma((n_ctx,)),
+            dma((n_ctx // 2,)),
+            dma((n_ctx // 2,)),
+            dma((n_ctx // 2,)),
+            dma((n_ctx // 2,)),
             dma((n_kvh, heads)),
             dma((n_kvh, heads)),
             dma((heads,)),
@@ -357,6 +443,9 @@
             pltpu.VMEM((n_kvh, heads, group * rows, 1), jnp.float32),
             pltpu.VMEM((n_kvh, heads, group * rows, 1), jnp.float32),
             pltpu.VMEM((n_kvh, heads, group * rows, hd), jnp.float32),
+            pltpu.VMEM(keys.shape, jnp.bfloat16),
+            dma((n_kvh,)),
+            dma((n_kvh,)),
         ],
         compiler_params=pltpu.CompilerParams(
             collective_id=0, has_side_effects=True, vmem_limit_bytes=64 * 1024 * 1024

time: 38.4 us -> 37.6 us (0.979)
  the two profiles are of different devices: /device:TPU:27 before, /device:TPU:25 now
where the time goes in v7:
time: 37.6 us; the launch traced here: 37.5 us
  Pallas kernels  35.4 us (94%)
  local copies, waits for them, and re-layouts  2.06 us (5%)
    pallas_call x1, Pallas kernels, per_device(): pl.pallas_call(functools.partial(kernel, n_ctx, n_kvh), out_shape=jax.Sha...  35.4 us
    unnamed x1, local copies, waits for them, and re-layouts  2.06 us

profile of v7, /device:TPU:25, one launch (start us, length us, event | category | flops | bytes accessed | tf_op | source)
XLA Modules:
  0.0 37.5 jit_solution(15809669502126236122)
XLA Ops:
  0.0 35.4 %shard_map.55 = bf16[96,4096]{1,0:T(8,128)(2,1)} custom-call(s32[2,4]{1,0:T(2,128)} %vert_hbm.1, s32[2,3]{1,0:T(2,128)} %offs_hbm.1, bf16[384,1024]{1,0:T(8,128)(2,1)} %q_hbm.1, bf16[384,256]{1,0:T(8,128)(2,1)} %k_hbm.1, bf16[384,256]{1,0:T(8,128)(2,1)} %v_hbm.1), custom_call_target="tpu_custom_call" | custom-call | tf_op jit(solution)/shard_map/pallas_call | solution.py:417
  35.4 2.1 %copy.7 = bf16[96,4096]{1,0:T(8,128)(2,1)} copy(bf16[96,4096]{1,0:T(8,128)(2,1)} %shard_map.55) | data formatting | bytes 1572864

commit v8 on v6

--- a/solution.py
+++ b/solution.py
@@ -148,13 +148,13 @@
             device_id_type=MESH,
         )
 
+    each(n_ctx - 1, lambda i: vert_copy(i).start())
+
     @pl.when(c < n_ctx - 1)
     def _():
         for chunk in reversed(range(n_kvh)):
             for which in range(2):
                 kv_copy(which, chunk).start()
-
-    each(n_ctx - 1, lambda i: vert_copy(i).start())
 
     @pl.when(c == 0)
     def _():

time: 38.4 us -> 39.4 us (1.026)
  the two profiles are of different devices: /device:TPU:27 before, /device:TPU:17 now
where the time goes in v8:
time: 39.4 us; the launch traced here: 39.2 us
  Pallas kernels  37.1 us (94%)
  local copies, waits for them, and re-layouts  2.06 us (5%)
    pallas_call x1, Pallas kernels, per_device(): pl.pallas_call(functools.partial(kernel, n_ctx, n_kvh), out_shape=jax.Sha...  37.1 us
    unnamed x1, local copies, waits for them, and re-layouts  2.06 us

profile of v8, /device:TPU:17, one launch (start us, length us, event | category | flops | bytes accessed | tf_op | source)
XLA Modules:
  0.0 39.2 jit_solution(4773205490519720307)
XLA Ops:
  0.0 37.1 %shard_map.55 = bf16[96,4096]{1,0:T(8,128)(2,1)} custom-call(s32[2,4]{1,0:T(2,128)} %vert_hbm.1, s32[2,3]{1,0:T(2,128)} %offs_hbm.1, bf16[384,1024]{1,0:T(8,128)(2,1)} %q_hbm.1, bf16[384,256]{1,0:T(8,128)(2,1)} %k_hbm.1, bf16[384,256]{1,0:T(8,128)(2,1)} %v_hbm.1), custom_call_target="tpu_custom_call" | custom-call | tf_op jit(solution)/shard_map/pallas_call | solution.py:333
  37.1 2.1 %copy.7 = bf16[96,4096]{1,0:T(8,128)(2,1)} copy(bf16[96,4096]{1,0:T(8,128)(2,1)} %shard_map.55) | data formatting | bytes 1572864

commit v9 on v4

--- a/solution.py
+++ b/solution.py
@@ -257,17 +257,17 @@
             )
             exp_w = jnp.exp2((score_w - top) * factor)
             exp_v = jnp.exp2((score_v - top) * factor)
-            total = jnp.sum(exp_w, axis=-1, keepdims=True) + jnp.sum(exp_v, axis=-1, keepdims=True)
             blended = jnp.dot(
                 exp_w.astype(jnp.bfloat16).reshape(group * rows, span),
-                vals,
+                jnp.concatenate([vals, jnp.ones_like(vals)], axis=1),
                 preferred_element_type=jnp.float32,
             ) + jnp.dot(
                 exp_v.astype(jnp.bfloat16).reshape(group * rows, slots * BLK),
-                vert_v[g],
+                jnp.concatenate([vert_v[g], jnp.ones_like(vert_v[g])], axis=1),
                 preferred_element_type=jnp.float32,
             )
-            result = (blended.reshape(group, rows, hd) / total).astype(jnp.bfloat16)
+            result = (blended[:, :hd] / blended[:, hd:]).astype(jnp.bfloat16)
+            result = result.reshape(group, rows, hd)
             for h in range(group):
                 obuf[base : base + rows, (g * group + h) * hd : (g * group + h + 1) * hd] = result[h]
 

time: 36.3 us -> 36.2 us (level)
  no operation moved by 1% of the time
where the time goes in v9:
time: 36.2 us; the launch traced here: 36 us
  Pallas kernels  34 us (94%)
  local copies, waits for them, and re-layouts  2.06 us (6%)
    pallas_call x1, Pallas kernels, per_device(): pl.pallas_call(functools.partial(kernel, n_ctx, n_kvh), out_shape=jax.Sha...  34 us
    unnamed x1, local copies, waits for them, and re-layouts  2.06 us

profile of v9, /device:TPU:16, one launch (start us, length us, event | category | flops | bytes accessed | tf_op | source)
XLA Modules:
  0.0 36.0 jit_solution(4501809019507774603)
XLA Ops:
  0.0 34.0 %shard_map.55 = bf16[96,4096]{1,0:T(8,128)(2,1)} custom-call(s32[2,4]{1,0:T(2,128)} %vert_hbm.1, s32[2,3]{1,0:T(2,128)} %offs_hbm.1, bf16[384,1024]{1,0:T(8,128)(2,1)} %q_hbm.1, bf16[384,256]{1,0:T(8,128)(2,1)} %k_hbm.1, bf16[384,256]{1,0:T(8,128)(2,1)} %v_hbm.1), custom_call_target="tpu_custom_call" | custom-call | tf_op jit(solution)/shard_map/pallas_call | solution.py:310
  34.0 2.1 %copy.7 = bf16[96,4096]{1,0:T(8,128)(2,1)} copy(bf16[96,4096]{1,0:T(8,128)(2,1)} %shard_map.55) | data formatting | bytes 1572864

commit v10 on v4

--- a/solution.py
+++ b/solution.py
@@ -311,7 +311,7 @@
         functools.partial(kernel, n_ctx, n_kvh),
         out_shape=jax.ShapeDtypeStruct((rows, queries.shape[1] * n_kvh), jnp.bfloat16),
         in_specs=[hbm] * 5,
-        out_specs=pl.BlockSpec(memory_space=pltpu.VMEM),
+        out_specs=hbm,
         scratch_shapes=[
             pltpu.SMEM(vertical.shape, jnp.int32),
             pltpu.SMEM(offsets.shape, jnp.int32),

time: 36.3 us -> 35.5 us (0.978)
  Pallas kernels: 34 us -> 33.2 us
    pallas_call x1, Pallas kernels: 34 us -> 33.2 us  [per_device(): pl.pallas_call(functools.partial(kernel, n_ctx, n_kvh), out_shape=jax.Sha...]
where the time goes in v10:
time: 35.5 us; the launch traced here: 35.3 us
  Pallas kernels  33.2 us (94%)
  local copies, waits for them, and re-layouts  2.06 us (6%)
    pallas_call x1, Pallas kernels, per_device(): pl.pallas_call(functools.partial(kernel, n_ctx, n_kvh), out_shape=jax.Sha...  33.2 us
    unnamed x1, local copies, waits for them, and re-layouts  2.06 us

profile of v10, /device:TPU:16, one launch (start us, length us, event | category | flops | bytes accessed | tf_op | source)
XLA Modules:
  0.0 35.3 jit_solution(1672439963343512277)
XLA Ops:
  0.0 33.2 %shard_map.55 = bf16[96,4096]{1,0:T(8,128)(2,1)} custom-call(s32[2,4]{1,0:T(2,128)} %vert_hbm.1, s32[2,3]{1,0:T(2,128)} %offs_hbm.1, bf16[384,1024]{1,0:T(8,128)(2,1)} %q_hbm.1, bf16[384,256]{1,0:T(8,128)(2,1)} %k_hbm.1, bf16[384,256]{1,0:T(8,128)(2,1)} %v_hbm.1), custom_call_target="tpu_custom_call" | custom-call | tf_op jit(solution)/shard_map/pallas_call | solution.py:310
  33.3 2.1 %copy.7 = bf16[96,4096]{1,0:T(8,128)(2,1)} copy(bf16[96,4096]{1,0:T(8,128)(2,1)} %shard_map.55) | data formatting | bytes 1572864
